TPU v7x, 32 devices: a whole 2x2x4 slice. The times are simulated.
32 devices in a mesh: fsdp: 8 (over y, x, core), tp: 4 (over z).
Axes of the slice: x: 2, y: 2, z: 4, core: 2. Of those that a mesh axis runs over, the one named last changes fastest.
Arguments:
- tokens: bfloat16 [16, 1024, 1024], P('fsdp', 'tp'), may hold values from -6 to 6
- lengths: int32 [16], replicated, may hold values from 1 to 1024, 10240 in all
- perm: int32 [16], replicated, may hold values from 0 to 15, as said below
- cotangent: bfloat16 [16, 1024, 1024], P('fsdp', 'tp'), may hold values from -6 to 6
- norm1_gain: float32 [1024], replicated, may hold values from 0.5 to 1.5
- input_weight: bfloat16 [1024, 8, 771], P('fsdp', 'tp'), may hold values from -0.1875 to 0.1875
- conv_w: float32 [8, 640, 4], replicated, may hold values from -3 to 3
- decay_log: float32 [8], replicated, may hold values from -7 to -2
- decay_bias: float32 [8], replicated, may hold values from -1 to 1
- out_gain: float32 [128], replicated, may hold values from 0.5 to 1.5
- w_out: bfloat16 [1024, 1024], P('tp', 'fsdp'), may hold values from -0.1875 to 0.1875
- norm2_gain: float32 [1024], replicated, may hold values from 0.5 to 1.5
- gate_up_weight: bfloat16 [1024, 2, 2816], P('fsdp', None, 'tp'), may hold values from -0.1875 to 0.1875
- down_weight: bfloat16 [2816, 1024], P('tp', 'fsdp'), may hold values from -0.109375 to 0.109375
Outputs:
- output: bfloat16 [16, 1024, 1024], P('fsdp', 'tp')
- input_grad: bfloat16 [16, 1024, 1024], P('fsdp', 'tp')
- grad_norm1_gain: float32 [1024], replicated
- grad_w_in: float32 [1024, 8, 771], P('fsdp', 'tp')
- grad_conv_w: float32 [8, 640, 4], replicated
- grad_decay_log: float32 [8], replicated
- grad_decay_bias: float32 [8], replicated
- grad_out_gain: float32 [128], replicated
- grad_w_out: float32 [1024, 1024], P('tp', 'fsdp')
- grad_norm2_gain: float32 [1024], replicated
- grad_w_gate_up: float32 [1024, 2, 2816], P('fsdp', None, 'tp')
- grad_w_down: float32 [2816, 1024], P('tp', 'fsdp')
Inputs may be any that keep to these rules, and one draw needn't show every extreme that they name: lengths[i] is the number of live tokens of sequence i; one sequence has exactly 1024. perm is a permutation; slot d belongs to index d // 2 of fsdp. The sequences of one index of fsdp (given order) go to 2 different indices, and each index receives at most one sequence from each index.
All inputs are finite; a program needn't handle non-finite values.
Results may differ from a plain program's by a relative error of at most 0.03.
Values may be sent and summed in bfloat16 or wider, within the bound.
No kernel may reach another device: no remote copies, remote signals or barrier semaphores. Data moves between devices by JAX's collectives and lax.ppermute only.
A program may use at most 320 MiB of HBM per device.

v0:
```python
import jax
import jax.numpy as jnp
from jax import lax
from jax.sharding import PartitionSpec as P

HEAD_DIM = 128
NH = 2
SPAN = 64
EPS_NORM = 1e-05
EPS_UNIT = 1e-06
PRECISION_MAX = lax.Precision.HIGHEST


def rms_scale(value, gain):
    return value * lax.rsqrt(jnp.mean(value * value, axis=-1, keepdims=True) + EPS_NORM) * gain


def unit_norm(value):
    return value * lax.rsqrt(jnp.sum(value * value, axis=-1, keepdims=True) + EPS_UNIT)


def causal_conv(raw_values, kernel):
    kernel_len = kernel.shape[-1]
    seq_len = raw_values.shape[1]
    padded = jnp.pad(raw_values, ((0, 0), (kernel_len - 1, 0), (0, 0), (0, 0)))
    summed = jnp.zeros_like(raw_values)
    for offset in range(kernel_len):
        summed = summed + padded[:, offset : offset + seq_len] * kernel[:, :, offset]
    return summed


def carry_step(state, pieces):
    weighted_block, value_block, key_block, decay_block = pieces
    updates = value_block - jnp.einsum("shid,shdv->shiv", key_block, state, precision=PRECISION_MAX)
    carried = decay_block * state + jnp.einsum(
        "shjd,shjv->shdv", weighted_block, updates, precision=PRECISION_MAX
    )
    return (carried, (state, updates))


def delta_product(queries, key_rows, values, beta_rows, log_decay):
    batch_seqs, seq_len, head_count, head_dim = queries.shape
    value_dim = values.shape[-1]
    blocks = seq_len // SPAN
    sub_decay = jnp.concatenate([log_decay[..., None], jnp.zeros_like(beta_rows[..., 1:])], axis=-1)

    def split_steps(value):
        tail_dims = value.shape[4:]
        shaped = value.reshape((batch_seqs, blocks, SPAN, head_count, NH) + tail_dims)
        axes_order = (1, 0, 3, 2, 4) + tuple(range(5, 5 + len(tail_dims)))
        return shaped.transpose(axes_order).reshape(
            (blocks, batch_seqs, head_count, SPAN * NH) + tail_dims
        )

    block_queries = queries.reshape(batch_seqs, blocks, SPAN, head_count, head_dim).transpose(
        1, 0, 3, 2, 4
    )
    block_keys = split_steps(key_rows)
    block_values = split_steps(values)
    block_betas = split_steps(beta_rows)
    cumulative = jnp.cumsum(split_steps(sub_decay), axis=-1)
    steps_in = SPAN * NH
    row_ids = lax.broadcasted_iota(jnp.int32, (steps_in, steps_in), 0)
    col_ids = lax.broadcasted_iota(jnp.int32, (steps_in, steps_in), 1)
    strictly = col_ids < row_ids
    key_inner = jnp.einsum("nshid,nshjd->nshij", block_keys, block_keys, precision=PRECISION_MAX)
    spread_log = cumulative[..., :, None] - cumulative[..., None, :]
    fading = jnp.where(strictly, jnp.exp(jnp.where(strictly, spread_log, 0.0)), 0.0)
    lower_mat = key_inner * fading * block_betas[..., :, None]
    right_sides = jnp.concatenate(
        [
            block_betas[..., None] * block_values,
            (block_betas * jnp.exp(cumulative))[..., None] * block_keys,
        ],
        axis=-1,
    )
    solved = jax.scipy.linalg.solve_triangular(
        lower_mat, right_sides, lower=True, unit_diagonal=True
    )
    value_part = solved[..., :value_dim]
    key_part = solved[..., value_dim:]
    last_log = cumulative[..., -1:]
    weighted = block_keys * jnp.exp(last_log - cumulative)[..., None]
    block_decay = jnp.exp(last_log)[..., None]
    first_state = jnp.zeros((batch_seqs, head_count, head_dim, value_dim), jnp.float32)
    last_state, (entering, updates) = lax.scan(
        carry_step, first_state, (weighted, value_part, key_part, block_decay)
    )
    read_log = cumulative[..., NH - 1 :: NH]
    out_rows = lax.broadcasted_iota(jnp.int32, (SPAN, steps_in), 0)
    out_cols = lax.broadcasted_iota(jnp.int32, (SPAN, steps_in), 1)
    visible = out_cols <= out_rows * NH + NH - 1
    query_key = jnp.einsum("nshid,nshjd->nshij", block_queries, block_keys, precision=PRECISION_MAX)
    read_spread = read_log[..., :, None] - cumulative[..., None, :]
    read_fade = jnp.where(visible, jnp.exp(jnp.where(visible, read_spread, 0.0)), 0.0)
    from_state = jnp.einsum("nshid,nshdv->nshiv", block_queries, entering, precision=PRECISION_MAX)
    outputs = jnp.exp(read_log)[..., None] * from_state + jnp.einsum(
        "nshij,nshjv->nshiv", query_key * read_fade, updates, precision=PRECISION_MAX
    )
    return outputs.transpose(1, 0, 3, 2, 4).reshape(batch_seqs, seq_len, head_count, value_dim)


def mixer_inner(projected_rows, conv_part, log_part, bias_part, out_gain):
    batch_seqs, seq_len, head_count, _ = projected_rows.shape
    conv_ch = conv_part.shape[1]
    conv_out = jax.nn.silu(causal_conv(projected_rows[..., :conv_ch], conv_part))
    queries = unit_norm(conv_out[..., :HEAD_DIM])
    key_rows = unit_norm(
        conv_out[..., HEAD_DIM : HEAD_DIM * (1 + NH)].reshape(
            batch_seqs, seq_len, head_count, NH, HEAD_DIM
        )
    )
    values = conv_out[..., HEAD_DIM * (1 + NH) :].reshape(
        batch_seqs, seq_len, head_count, NH, HEAD_DIM
    )
    out_gate = projected_rows[..., conv_ch : conv_ch + HEAD_DIM]
    beta_rows = jax.nn.sigmoid(projected_rows[..., conv_ch + HEAD_DIM : conv_ch + HEAD_DIM + NH])
    log_decay = -jnp.exp(log_part) * jax.nn.softplus(
        projected_rows[..., conv_ch + HEAD_DIM + NH] + bias_part
    )
    result = delta_product(queries, key_rows, values, beta_rows, log_decay)
    return rms_scale(result, out_gain) * jax.nn.silu(out_gate)


def swiglu(gate_up_result):
    return jax.nn.silu(gate_up_result[..., 0, :]) * gate_up_result[..., 1, :]


def spread(value):
    return lax.all_gather(value, "tp", axis=1, tiled=True)


def collect(value):
    return lax.psum_scatter(
        value.astype(jnp.bfloat16), "tp", scatter_dimension=1, tiled=True
    ).astype(jnp.float32)


def spread_back(value):
    return lax.all_gather(value, "tp", axis=1, tiled=True)


def collect_back(value):
    return lax.psum_scatter(
        value.astype(jnp.bfloat16), "tp", scatter_dimension=1, tiled=True
    ).astype(jnp.float32)


def local(
    tokens,
    lengths,
    perm,
    cotangent,
    norm1_gain,
    input_weight,
    conv_w,
    decay_log,
    decay_bias,
    out_gain,
    w_out,
    norm2_gain,
    gate_up_weight,
    down_weight,
):
    group_count = lax.axis_size("fsdp")
    own_group = lax.axis_index("fsdp")
    tensor_pos = lax.axis_index("tp")
    slot_count = tokens.shape[0]
    piece_len = tokens.shape[1]
    sources = perm.reshape(group_count, slot_count)
    local_ids = jnp.arange(slot_count, dtype=jnp.int32)
    group_ids = jnp.arange(group_count, dtype=jnp.int32)
    from_here = sources // slot_count == own_group
    matches = jnp.logical_and(
        from_here[:, :, None], (sources % slot_count)[:, :, None] == local_ids[None, None, :]
    )
    send_pick = jnp.sum(matches.astype(jnp.int32), axis=1).astype(jnp.bfloat16)
    sending = jnp.einsum(
        "gj,jtd->gtd", send_pick, tokens, preferred_element_type=jnp.float32
    ).astype(jnp.bfloat16)
    arrived = lax.all_to_all(sending, "fsdp", split_axis=0, concat_axis=0, tiled=True)
    my_sources = lax.dynamic_index_in_dim(sources, own_group, 0, keepdims=False)
    take_pick = ((my_sources // slot_count)[:, None] == group_ids[None, :]).astype(jnp.bfloat16)
    slot_tokens = jnp.einsum("sg,gtd->std", take_pick, arrived, preferred_element_type=jnp.float32)
    slot_len = jnp.take(lengths, my_sources)
    positions = tensor_pos * piece_len + jnp.arange(piece_len, dtype=jnp.int32)
    live_mask = (positions[None, :] < slot_len[:, None]).astype(jnp.float32)[..., None]
    head_count = input_weight.shape[1]
    head_start = tensor_pos * head_count
    conv_part = lax.dynamic_slice_in_dim(conv_w, head_start, head_count, 0)
    log_part = lax.dynamic_slice_in_dim(decay_log, head_start, head_count, 0)
    bias_part = lax.dynamic_slice_in_dim(decay_bias, head_start, head_count, 0)
    input_weight_whole, out_full = (
        lax.all_gather(input_weight, "fsdp", axis=0, tiled=True),
        lax.all_gather(w_out, "fsdp", axis=1, tiled=True),
    )
    model_dim = input_weight_whole.shape[0]
    output_matrix = out_full.reshape(head_count, HEAD_DIM, model_dim)
    normed_one = rms_scale(slot_tokens, norm1_gain).astype(jnp.bfloat16)
    gathered_first = spread(normed_one)
    projected_rows = jnp.einsum(
        "mzk,kin->mzin", gathered_first, input_weight_whole, preferred_element_type=jnp.float32
    )
    gated, inner_pull = jax.vjp(
        mixer_inner, projected_rows, conv_part, log_part, bias_part, out_gain
    )
    gated_reduced = gated.astype(jnp.bfloat16)
    mixer_result = jnp.einsum(
        "gtpo,poz->gtz", gated_reduced, output_matrix, preferred_element_type=jnp.float32
    )
    middle = slot_tokens + collect(mixer_result)
    gate_up_weight_whole, down_weight_whole = (
        lax.all_gather(gate_up_weight, "fsdp", axis=0, tiled=True),
        lax.all_gather(down_weight, "fsdp", axis=1, tiled=True),
    )
    normed_two = rms_scale(middle, norm2_gain).astype(jnp.bfloat16)
    gathered_second = spread(normed_two)
    gate_up_result = jnp.einsum(
        "tux,xeg->tueg", gathered_second, gate_up_weight_whole, preferred_element_type=jnp.float32
    )
    hidden_val, hidden_pull = jax.vjp(swiglu, gate_up_result)
    hidden_reduced = hidden_val.astype(jnp.bfloat16)
    forward_net_output = jnp.einsum(
        "wqh,hv->wqv", hidden_reduced, down_weight_whole, preferred_element_type=jnp.float32
    )
    block_out = live_mask * (middle + collect(forward_net_output))
    slot_cot = live_mask * cotangent.astype(jnp.float32)
    gradient_rows_second = spread_back(slot_cot.astype(jnp.bfloat16))
    grad_down = jnp.einsum(
        "kob,koi->bi", hidden_reduced, gradient_rows_second, preferred_element_type=jnp.float32
    )
    grad_hidden = jnp.einsum(
        "igx,bx->igb", gradient_rows_second, down_weight_whole, preferred_element_type=jnp.float32
    )
    gradient_couple = hidden_pull(grad_hidden)[0]
    grad_gate_up = jnp.einsum(
        "rzt,rzih->tih",
        gathered_second.astype(jnp.float32),
        gradient_couple,
        precision=PRECISION_MAX,
    )
    grad_normed_two = jnp.einsum(
        "uxmw,zmw->uxz",
        gradient_couple,
        gate_up_weight_whole.astype(jnp.float32),
        precision=PRECISION_MAX,
    )
    norm_pull_two = jax.vjp(rms_scale, middle, norm2_gain)[1]
    grad_mid_norm, grad_gain_two = norm_pull_two(collect_back(grad_normed_two))
    grad_middle = slot_cot + grad_mid_norm
    gradient_rows_first = spread_back(grad_middle.astype(jnp.bfloat16))
    grad_out = jnp.einsum(
        "irpy,irk->pyk", gated_reduced, gradient_rows_first, preferred_element_type=jnp.float32
    ).reshape(head_count * HEAD_DIM, model_dim)
    grad_gated = jnp.einsum(
        "ein,wcn->eiwc", gradient_rows_first, output_matrix, preferred_element_type=jnp.float32
    )
    gradient_projected, grad_conv, grad_log, grad_bias, grad_gain_out = inner_pull(grad_gated)
    grad_in = jnp.einsum(
        "bwg,bwfi->gfi",
        gathered_first.astype(jnp.float32),
        gradient_projected,
        precision=PRECISION_MAX,
    )
    grad_normed_one = jnp.einsum(
        "zqtv,btv->zqb",
        gradient_projected,
        input_weight_whole.astype(jnp.float32),
        precision=PRECISION_MAX,
    )
    norm_pull_one = jax.vjp(rms_scale, slot_tokens, norm1_gain)[1]
    grad_tok_norm, grad_gain_one = norm_pull_one(collect_back(grad_normed_one))
    input_slot = (grad_middle + grad_tok_norm).astype(jnp.bfloat16)
    grad_in, grad_out, grad_gate_up, grad_down = (
        lax.psum_scatter(
            grad_in.astype(jnp.bfloat16), "fsdp", scatter_dimension=0, tiled=True
        ).astype(jnp.float32),
        lax.psum_scatter(
            grad_out.astype(jnp.bfloat16), "fsdp", scatter_dimension=1, tiled=True
        ).astype(jnp.float32),
        lax.psum_scatter(
            grad_gate_up.astype(jnp.bfloat16), "fsdp", scatter_dimension=0, tiled=True
        ).astype(jnp.float32),
        lax.psum_scatter(
            grad_down.astype(jnp.bfloat16), "fsdp", scatter_dimension=1, tiled=True
        ).astype(jnp.float32),
    )
    conv_full = lax.dynamic_update_slice_in_dim(jnp.zeros_like(conv_w), grad_conv, head_start, 0)
    log_full = lax.dynamic_update_slice_in_dim(jnp.zeros_like(decay_log), grad_log, head_start, 0)
    bias_full = lax.dynamic_update_slice_in_dim(
        jnp.zeros_like(decay_bias), grad_bias, head_start, 0
    )
    small_sums = lax.psum(
        (grad_gain_one, grad_gain_two, conv_full, log_full, bias_full, grad_gain_out),
        ("fsdp", "tp"),
    )
    out_home = jnp.einsum(
        "sg,std->gtd", take_pick, block_out.astype(jnp.bfloat16), preferred_element_type=jnp.float32
    ).astype(jnp.bfloat16)
    grad_home = jnp.einsum(
        "sg,std->gtd", take_pick, input_slot, preferred_element_type=jnp.float32
    ).astype(jnp.bfloat16)
    back_out, back_grad = (
        lax.all_to_all(out_home, "fsdp", split_axis=0, concat_axis=0, tiled=True),
        lax.all_to_all(grad_home, "fsdp", split_axis=0, concat_axis=0, tiled=True),
    )
    output = jnp.einsum(
        "gj,gtd->jtd", send_pick, back_out, preferred_element_type=jnp.float32
    ).astype(jnp.bfloat16)
    input_grad = jnp.einsum(
        "gj,gtd->jtd", send_pick, back_grad, preferred_element_type=jnp.float32
    ).astype(jnp.bfloat16)
    return (
        output,
        input_grad,
        small_sums[0],
        grad_in,
        small_sums[2],
        small_sums[3],
        small_sums[4],
        small_sums[5],
        grad_out,
        small_sums[1],
        grad_gate_up,
        grad_down,
    )


def solution(mesh):
    return jax.shard_map(
        local,
        mesh=mesh,
        in_specs=(
            P("fsdp", "tp", None),
            P(),
            P(),
            P("fsdp", "tp", None),
            P(),
            P("fsdp", "tp", None),
            P(),
            P(),
            P(),
            P(),
            P("tp", "fsdp"),
            P(),
            P("fsdp", None, "tp"),
            P("tp", "fsdp"),
        ),
        out_specs=(
            P("fsdp", "tp", None),
            P("fsdp", "tp", None),
            P(),
            P("fsdp", "tp", None),
            P(),
            P(),
            P(),
            P(),
            P("tp", "fsdp"),
            P(),
            P("fsdp", None, "tp"),
            P("tp", "fsdp"),
        ),
        check_vma=False,
    )
```

profile of v0, /device:TPU:8, one launch (start us, length us, event | category | flops | bytes accessed | tf_op | source)
XLA Modules:
  0.0 2863.2 jit_solution(13583249474675545995)
XLA Ops:
  22.7 57.9 %all-to-all-done = bf16[8,256,1024]{2,1,0:T(8,128)(2,1)} async-done(((bf16[8,256,1024]{2,1,0:T(8,128)(2,1)}), bf16[8,256,1024]{2,1,0:T(8,128)(2,1)}, u32[]{:S(2)}, u32[]{:S(2)}) %all-to-all-start) | async-done | bytes 4194336 | tf_op jit(solution)/shard_map/all_to_all | solution.py:181
  99.7 65.8 %all-gather.8.cloned.1.call-done = bf16[2,1024,1024]{2,0,1:T(2,128)(2,1)} async-done(((bf16[2,256,1024]{2,0,1:T(2,128)(2,1)}), bf16[2,1024,1024]{2,0,1:T(2,128)(2,1)}) %all-gather.8.cloned.1.call-update) | async-done | bytes 4194320 | tf_op jit(solution)/shard_map/all_gather | solution.py:130
  165.6 12.8 fusion.63
  263.2 630.3 %custom-call.10 = f32[16,2,2,1,128,128]{4,5,3,2,1,0:T(8,128)} custom-call(f32[16,2,2,1,128,128]{5,4,3,2,1,0:T(8,128)} %get-tuple-element.727), custom_call_target="InvertDiagBlocksLowerTriangular" | custom-call | tf_op jit(solution)/shard_map/jvp(jit(_solve_triangular))/vmap(vmap(vmap()))/triangular_solve | solution.py:77
  925.0 81.9 %while.38 = (s32[]{:T(128)}, f32[2,2,128,128]{3,2,1,0:T(8,128)S(1)}, f32[16,2,2,128,128]{4,3,2,1,0:T(8,128)}, f32[16,2,2,128,128]{4,3,2,1,0:T(8,128)}, f32[16,2,...) while((s32[]{:T(128)}, ...), condition=%wide.region_6.7_spmd.clone, body=%wide.region_5.6_spmd.clone.sunk | while | flops 201719808 | bytes 2885797 | solution.py:86
  1059.3 152.3 %all-reduce.36.cloned.1.call-done = bf16[2,1024,1024]{2,0,1:T(2,128)(2,1)} async-done(((bf16[2,1024,1024]{2,0,1:T(2,128)(2,1)}), bf16[2,1024,1024]{2,0,1:T(2,128)(2,1)}) %all-reduce.36.cloned.1.call-update) | async-done | bytes 4194320
  1222.7 23.7 all-gather.14.cloned.1.call-done
  1246.4 80.2 %all-gather.12.cloned.1.call-done = bf16[2,1024,1024]{2,0,1:T(2,128)(2,1)} async-done(((bf16[2,256,1024]{2,0,1:T(2,128)(2,1)}), bf16[2,1024,1024]{2,0,1:T(2,128)(2,1)}) %all-gather.12.cloned.1.call-update) | async-done | bytes 4194320 | tf_op jit(solution)/shard_map/all_gather | solution.py:130
  1326.6 12.1 fusion.57
  1338.7 16.3 all-gather.16.cloned.1.call-done
  1355.0 80.4 %all-gather.18.cloned.1.call-done = bf16[2,1024,1024]{2,0,1:T(2,128)(2,1)} async-done(((bf16[2,256,1024]{2,0,1:T(2,128)(2,1)}), bf16[2,1024,1024]{2,0,1:T(2,128)(2,1)}) %all-gather.18.cloned.1.call-update) | async-done | bytes 4194320 | tf_op jit(solution)/shard_map/all_gather | solution.py:140
  1451.0 22.6 bitcast_convert_fusion.1
  1482.2 154.1 %all-reduce.38.cloned.1.call-done = bf16[2,1024,1024]{2,0,1:T(2,128)(2,1)} async-done(((bf16[2,1024,1024]{2,0,1:T(2,128)(2,1)}), bf16[2,1024,1024]{2,0,1:T(2,128)(2,1)}) %all-reduce.38.cloned.1.call-update) | async-done | bytes 4194320
  1673.8 57.9 %all-gather.20.cloned.1.call-done = bf16[2,1024,1024]{2,0,1:T(2,128)(2,1)} async-done(((bf16[2,256,1024]{2,0,1:T(2,128)(2,1)}), bf16[2,1024,1024]{2,0,1:T(2,128)(2,1)}) %all-gather.20.cloned.1.call-update) | async-done | bytes 4194320 | tf_op jit(solution)/shard_map/all_gather | solution.py:140
  1786.2 164.6 %while.39 = (s32[]{:T(128)}, f32[2,2,128,128]{3,2,1,0:T(8,128)S(1)}, f32[16,2,2,128,128]{4,3,2,1,0:T(8,128)}, f32[16,2,2,128,128]{4,3,2,1,0:T(8,128)}, f32[16,2,...) while((s32[]{:T(128)}, ...), condition=%wide.region_19.20_spmd.clone, body=%wide.region_17.19_spmd.clone.sunk | while | flops 403439616 | bytes 4726519 | solution.py:86
  1950.7 16.3 fusion.48
  1967.0 12.5 fusion.49
  1979.5 19.7 multiply_reduce_fusion.6
  1999.2 13.9 fusion.94
  2021.9 11.9 add_add_fusion.1
  2120.1 23.4 multiply_reduce_fusion.2
  2143.5 14.4 broadcast_multiply_fusion
  2157.9 16.2 pad_add_fusion.2
  2177.9 26.0 bitcast_convert_fusion
  2218.2 25.0 bitcast_convert_fusion.4
  2248.0 252.9 %all-reduce.40.cloned.1.call-done = (bf16[2,1024,1024]{2,0,1:T(2,128)(2,1)}, bf16[2,1024,1024]{2,0,1:T(2,128)(2,1)}) async-done(((bf16[2,1024,1024]{2,0,1:T(2,128)(2,1)}, bf16[2,1024,1024]{2,0,1:T(2,128)(2,1)}), (bf16[2,1024,1024]{2,0,1:T(2,128)(2,1)}, bf16[2,1024,1024]{2,0,1:T(2,128)(2,1)})) %all-reduce.40.cloned.1.call-update) | async-done | bytes 8388624
  2524.3 30.6 %bitcast_convert_fusion.3 = bf16[1024,2,771]{0,2,1:T(8,128)(2,1)} fusion(f32[2,1024,2,640]{1,3,2,0:T(8,128)} %copy-done.27, f32[2,1024,2,128]{1,3,2,0:T(8,128)} %get-tuple-element.701, f32[2,1024,2,2]{1,3,2,0:T(2,128)S(1)} %fusion.193, f32[2,1024,2,1]{1,3,2,0:T(1,128)S(1)} %get-tuple-element.703, bf16[2,1024,1024]{2,0,1:T(2,128)(2,1)} %all-gather.8.cloned.1.call-done), kind=kOutput, calls=%fused_computation.85 | convolution fusion | flops 38816751616 | bytes 19984384 | tf_op jit(solution)/shard_map/bwg,bwfi->gfi/dot_general | solution.py:259
  2581.2 56.3 %reduce-scatter.17.cloned.1.call-done = bf16[128,1408]{1,0:T(8,128)(2,1)} async-done(((bf16[1024,1408]{1,0:T(8,128)(2,1)}), bf16[128,1408]{1,0:T(8,128)(2,1)}) %reduce-scatter.17.cloned.1.call-update) | async-done | bytes 360464
  2641.2 33.5 %reduce-scatter.15.cloned.1.call-done = bf16[128,256]{1,0:T(8,128)(2,1)} async-done(((bf16[1024,256]{1,0:T(8,128)(2,1)}), bf16[128,256]{1,0:T(8,128)(2,1)}) %reduce-scatter.15.cloned.1.call-update) | async-done | bytes 65552
  2676.4 49.2 %reduce-scatter.13.cloned.1.call-done = bf16[128,1542]{1,0:T(8,128)(2,1)} async-done(((bf16[1024,1542]{1,0:T(8,128)(2,1)}), bf16[128,1542]{1,0:T(8,128)(2,1)}) %reduce-scatter.13.cloned.1.call-update) | async-done | bytes 394768
  2728.9 39.5 %all-reduce.27 = (f32[1024]{0:T(1024)}, f32[8]{0:T(128)}, f32[8]{0:T(128)}, f32[128]{0:T(128)}, f32[1024]{0:T(1024)}) all-reduce(f32[1024]{0:T(1024)S(1)} %get-tuple-element.632, f32[8]{0:T(128)S(1)} %multiply_dynamic-update-slice_fusion, f32[8]{0:T(128)S(1)} %dynamic_update_slice.55, ...), channel_id=1, replica_groups=mesh['fsdp'=8,'tp'=4] {'fsdp','tp'}, use_global_device_ids=true, to_apply=%region_33.34 | all-reduce | flops 2192 | bytes 17536 | tf_op jit(solution)/shard_map/psum | solution.py:293
  2780.9 74.0 %all-reduce.34.cloned.1.call-done = f32[8,640,4]{1,2,0:T(4,128)} async-done(((f32[8,640,4]{1,2,0:T(4,128)}), f32[8,640,4]{1,2,0:T(4,128)}) %all-reduce.34.cloned.1.call-update) | async-done | bytes 81936 | tf_op jit(solution)/shard_map/psum | solution.py:293
  (633 shorter events, 764.3 us)
Async XLA Ops:
  7.2 92.5 %all-gather.10.cloned.1.call-start = ((), (), s32[]{:S(2)}) async-start(), calls=%async_computation.8 | async-start | bytes 3575808 | tf_op jit(solution)/shard_map/all_gather | solution.py:194
  16.7 63.9 %all-to-all-start = ((bf16[8,256,1024]{2,1,0:T(8,128)(2,1)}), bf16[8,256,1024]{2,1,0:T(8,128)(2,1)}, u32[]{:S(2)}, u32[]{:S(2)}) async-start(bf16[8,256,1024]{2,1,0:T(8,128)(2,1)} %copy.605), calls=%async_computation | async-start | bytes 8388608 | tf_op jit(solution)/shard_map/all_to_all | solution.py:181
  21.4 144.1 %all-gather.8.cloned.1.call-start = ((), (), s32[]{:S(2)}) async-start(), calls=%async_computation.7 | async-start | bytes 5242880 | tf_op jit(solution)/shard_map/all_gather | solution.py:130
  88.0 1123.6 %all-reduce.36.cloned.1.call-start = ((), (), s32[]{:S(2)}) async-start(), calls=%async_computation.19 | async-start | bytes 8388608
  205.8 713.6 %copy-start.81 = (f32[16,2,2,1]{0,2,3,1:T(2,128)}, f32[16,2,2,1]{0,2,3,1:T(2,128)S(1)}, u32[]{:S(2)}) copy-start(f32[16,2,2,1]{0,2,3,1:T(2,128)S(1)} %copy.768) | copy-start | bytes 772
  207.7 799.3 %copy-start.54 = (f32[2,1024,2]{1,2,0:T(2,128)}, f32[2,1024,2]{1,2,0:T(2,128)S(1)}, u32[]{:S(2)}) copy-start(f32[2,1024,2]{1,2,0:T(2,128)S(1)} %multiply_reduce_fusion.14) | copy-start | bytes 49156
  208.6 820.7 %copy-start.39 = (f32[16,2,2,64]{0,2,3,1:T(2,128)}, f32[16,2,2,64]{0,2,3,1:T(2,128)S(1)}, u32[]{:S(2)}) copy-start(f32[16,2,2,64]{0,2,3,1:T(2,128)S(1)} %copy.614) | copy-start | bytes 49156
  255.0 638.7 %copy-start.28 = (f32[2,16,64,2,2]{1,4,2,3,0:T(2,128)}, f32[2,16,64,2,2]{1,4,2,3,0:T(2,128)S(1)}, u32[]{:S(2)}) copy-start(f32[2,16,64,2,2]{1,4,2,3,0:T(2,128)S(1)} %copy.626) | copy-start | bytes 98308
  1057.4 157.7 %copy-start.78 = (f32[1024]{0:T(1024)S(1)}, f32[1024]{0:T(1024)}, u32[]{:S(2)}) copy-start(f32[1024]{0:T(1024)} %param.29) | copy-start | bytes 12292
  1057.5 188.9 %all-gather.14.cloned.1.call-start = ((), (), s32[]{:S(2)}) async-start(), calls=%async_computation.10 | async-start | bytes 3244032 | tf_op jit(solution)/shard_map/all_gather | solution.py:213
  1058.0 268.5 %all-gather.12.cloned.1.call-start = ((), (), s32[]{:S(2)}) async-start(), calls=%async_computation.9 | async-start | bytes 5242880 | tf_op jit(solution)/shard_map/all_gather | solution.py:130
  1059.3 160.5 %copy-start.30 = (bf16[2,256,1024]{2,1,0:T(8,128)(2,1)S(1)}, bf16[2,256,1024]{2,1,0:T(8,128)(2,1)}, u32[]{:S(2)}) copy-start(bf16[2,256,1024]{2,1,0:T(8,128)(2,1)} %param.21) | copy-start | bytes 3145732
  1214.9 430.2 %copy-start.9 = (f32[2,256,1024]{2,0,1:T(2,128)}, f32[2,256,1024]{2,0,1:T(2,128)S(1)}, u32[]{:S(2)}) copy-start(f32[2,256,1024]{2,0,1:T(2,128)S(1)} %get-tuple-element.692) | copy-start | bytes 6291460
  1217.1 137.9 %all-gather.16.cloned.1.call-start = ((), (), s32[]{:S(2)}) async-start(), calls=%async_computation.11 | async-start | bytes 1622016 | tf_op jit(solution)/shard_map/all_gather | solution.py:214
  1217.7 217.7 %all-gather.18.cloned.1.call-start = ((), (), s32[]{:S(2)}) async-start(), calls=%async_computation.12 | async-start | bytes 5242880 | tf_op jit(solution)/shard_map/all_gather | solution.py:140
  1219.9 425.3 %copy-start.35 = (f32[2,256]{0,1:T(8,128)}, f32[2,256]{0,1:T(8,128)S(1)}, u32[]{:S(2)}) copy-start(f32[2,256]{0,1:T(8,128)S(1)} %copy.603) | copy-start | bytes 6148
  1222.6 413.6 %all-reduce.38.cloned.1.call-start = ((), (), s32[]{:S(2)}) async-start(), calls=%async_computation.20 | async-start | bytes 8388608
  1482.1 249.5 %all-gather.20.cloned.1.call-start = ((), (), s32[]{:S(2)}) async-start(), calls=%async_computation.13 | async-start | bytes 5242880 | tf_op jit(solution)/shard_map/all_gather | solution.py:140
  1652.2 848.7 %all-reduce.40.cloned.1.call-start = ((), (), s32[]{:S(2)}) async-start(), calls=%async_computation.21 | async-start | bytes 16777216
  2210.2 369.1 %reduce-scatter.19.cloned.1.call-start = ((), (), s32[]{:S(2)}) async-start(), calls=%async_computation.18 | async-start | bytes 1769472
  2218.1 419.4 %reduce-scatter.17.cloned.1.call-start = ((), (), s32[]{:S(2)}) async-start(), calls=%async_computation.17 | async-start | bytes 3244032
  2243.2 257.7 %copy-start.21 = (f32[2,256,1024]{2,0,1:T(2,128)S(1)}, f32[2,256,1024]{2,0,1:T(2,128)}, u32[]{:S(2)}) copy-start(f32[2,256,1024]{2,0,1:T(2,128)} %copy-done.20) | copy-start | bytes 6291460
  2243.2 257.7 %copy-start.38 = (f32[2,256]{0,1:T(8,128)S(1)}, f32[2,256]{0,1:T(8,128)}, u32[]{:S(2)}) copy-start(f32[2,256]{0,1:T(8,128)} %copy-done.37) | copy-start | bytes 6148
  2243.2 257.7 %copy-start.84 = (f32[1024]{0:T(1024)S(1)}, f32[1024]{0:T(1024)}, u32[]{:S(2)}) copy-start(f32[1024]{0:T(1024)} %param.22) | copy-start | bytes 12292
  2248.0 257.0 %copy-start.80 = (f32[2,256]{1,0:T(2,128)S(1)}, f32[2,256]{1,0:T(2,128)}, u32[]{:S(2)}) copy-start(f32[2,256]{1,0:T(2,128)} %copy-done.79) | copy-start | bytes 6148
  2248.0 257.1 %copy-start.93 = (s32[2]{0:T(128)S(1)}, s32[2]{0:T(128)}, u32[]{:S(2)}) copy-start(s32[2]{0:T(128)} %copy-done.92) | copy-start | bytes 28
  2514.4 60.2 %all-to-all-start.2 = ((bf16[8,256,1024]{2,1,0:T(8,128)(2,1)}), bf16[8,256,1024]{2,1,0:T(8,128)(2,1)}, u32[]{:S(2)}, u32[]{:S(2)}) async-start(bf16[8,256,1024]{2,1,0:T(8,128)(2,1)} %copy.709), calls=%async_computation.2 | async-start | bytes 8388608 | tf_op jit(solution)/shard_map/all_to_all | solution.py:305
  2519.2 155.6 %reduce-scatter.15.cloned.1.call-start = ((), (), s32[]{:S(2)}) async-start(), calls=%async_computation.16 | async-start | bytes 589824
  2524.1 201.5 %reduce-scatter.13.cloned.1.call-start = ((), (), s32[]{:S(2)}) async-start(), calls=%async_computation.15 | async-start | bytes 3833856
  2574.6 198.8 %all-to-all-start.1 = ((bf16[8,256,1024]{2,1,0:T(8,128)(2,1)}), bf16[8,256,1024]{2,1,0:T(8,128)(2,1)}, u32[]{:S(2)}, u32[]{:S(2)}) async-start(bf16[8,256,1024]{2,1,0:T(8,128)(2,1)} %copy.650), calls=%async_computation.1 | async-start | bytes 8388608 | tf_op jit(solution)/shard_map/all_to_all | solution.py:304
  2579.3 189.1 %copy-start.87 = (s32[8,2]{0,1:T(2,128)S(1)}, s32[8,2]{0,1:T(2,128)}, u32[]{:S(2)}) copy-start(s32[8,2]{0,1:T(2,128)} %copy-done.86) | copy-start | bytes 196
  2579.3 275.6 %all-reduce.34.cloned.1.call-start = ((), (), s32[]{:S(2)}) async-start(), calls=%async_computation.14 | async-start | bytes 163840 | tf_op jit(solution)/shard_map/psum | solution.py:293
  (92 other events, 2356.4 us)
Sparse Core Ops, SparseCore 0:
  10.5 58.4 all-gather.9
  88.2 77.3 all-gather.7
  1057.6 153.9 all-reduce.35
  1213.5 32.8 all-gather.13
  1248.4 78.1 all-gather.11
  1328.5 26.4 all-gather.15
  1357.2 78.1 all-gather.17
  1482.2 153.9 all-reduce.37
  1652.3 79.2 all-gather.19
  2210.3 290.5 all-reduce.39
  2504.2 51.8 reduce-scatter.18
  2559.3 78.1 reduce-scatter.16
  2641.5 33.2 reduce-scatter.14
  2678.1 47.4 reduce-scatter.12
  2732.5 122.3 all-reduce.33
where the time goes:
time: 2880 us; the launch traced here: 2860 us
  waiting for transfers between devices  1160 us (40%)
  other arithmetic  816 us (28%)
  matrix products  569 us (20%)
  local copies, waits for them, and re-layouts  238 us (8%)
  blocking collectives  49.6 us (2%)
    unnamed x22, waiting for transfers between devices  700 us
    another operation x4, other arithmetic, delta_product(): jax.scipy.linalg.solve_triangular(lower_mat, right_sides, lower=True, uni...  638 us
    all_gather x2, waiting for transfers between devices, spread(): return lax.all_gather(value, 'tp', axis=1, tiled=True)  146 us
    all_gather x2, waiting for transfers between devices, spread_back(): return lax.all_gather(value, 'tp', axis=1, tiled=True)  138 us
    dot_general x48, matrix products, carry_step(): jnp.einsum('shid,shdv->shiv', key_block, state, precision=PRECISION_MAX)  98.7 us
    dot_general x48, matrix products, carry_step(): jnp.einsum('shjd,shjv->shdv', weighted_block, updates, precision=PRECISIO...  96.4 us
    psum x1, waiting for transfers between devices, local(): lax.psum((grad_gain_one, grad_gain_two, conv_full, log_full, bias_full, g...  74 us
    all_to_all x1, waiting for transfers between devices, local(): lax.all_to_all(sending, 'fsdp', split_axis=0, concat_axis=0, tiled=True)  57.9 us
  transfers between devices with their start and end apart: 18, of which 15 were waited for; matrix products, arithmetic and copies ran while one was open for 7% of the time, Pallas kernels for 0%

commit v1 on v0

--- a/solution.py
+++ b/solution.py
@@ -127,7 +127,9 @@
 
 
 def spread(value):
-    return lax.all_gather(value, "tp", axis=1, tiled=True)
+    return jnp.concatenate(
+        lax.all_to_all(jnp.stack([value] * lax.axis_size("tp")), "tp", 0, 0), axis=1
+    )
 
 
 def collect(value):

time: 2880 us -> 2830 us (0.983)
  waiting for transfers between devices: 1160 us -> 1110 us
    all_to_all x0 -> x2, waiting for transfers between devices: none -> 216 us  [spread(): lax.all_to_all(jnp.stack([value] * lax.axis_size('tp')), 'tp', 0, 0)]
    all_gather x2 -> x0, waiting for transfers between devices: 146 us -> none  [spread(): return lax.all_gather(value, 'tp', axis=1, tiled=True)]
    all_gather x2, waiting for transfers between devices: 138 us -> 57.9 us  [spread_back(): return lax.all_gather(value, 'tp', axis=1, tiled=True)]
    unnamed x22 -> x20, waiting for transfers between devices: 700 us -> 704 us
  transfers between devices with their start and end apart: 18 -> 18, of which waited for: 15 -> 12; matrix products, arithmetic and copies ran while one was open for 7% -> 6% of each run, Pallas kernels for 0% -> 0%
where the time goes in v1:
time: 2830 us; the launch traced here: 2820 us
  waiting for transfers between devices  1110 us (39%)
  other arithmetic  811 us (29%)
  matrix products  560 us (20%)
  local copies, waits for them, and re-layouts  243 us (9%)
  blocking collectives  49.6 us (2%)
  starting transfers between devices  28.3 us (1%)
    unnamed x20, waiting for transfers between devices  704 us
    another operation x4, other arithmetic, delta_product(): jax.scipy.linalg.solve_triangular(lower_mat, right_sides, lower=True, uni...  638 us
    all_to_all x2, waiting for transfers between devices, spread(): lax.all_to_all(jnp.stack([value] * lax.axis_size('tp')), 'tp', 0, 0)  216 us
    dot_general x48, matrix products, carry_step(): jnp.einsum('shid,shdv->shiv', key_block, state, precision=PRECISION_MAX)  98.8 us
    dot_general x48, matrix products, carry_step(): jnp.einsum('shjd,shjv->shdv', weighted_block, updates, precision=PRECISIO...  96.4 us
    psum x1, waiting for transfers between devices, local(): lax.psum((grad_gain_one, grad_gain_two, conv_full, log_full, bias_full, g...  74.1 us
    all_gather x2, waiting for transfers between devices, spread_back(): return lax.all_gather(value, 'tp', axis=1, tiled=True)  57.9 us
  transfers between devices with their start and end apart: 18, of which 12 were waited for; matrix products, arithmetic and copies ran while one was open for 6% of the time, Pallas kernels for 0%

profile of v1, /device:TPU:8, one launch (start us, length us, event | category | flops | bytes accessed | tf_op | source)
XLA Modules:
  0.0 2817.3 jit_solution(14211982804223610890)
XLA Ops:
  20.2 48.4 %all-to-all-done = bf16[8,256,1024]{2,1,0:T(8,128)(2,1)} async-done(((bf16[8,256,1024]{2,1,0:T(8,128)(2,1)}), bf16[8,256,1024]{2,1,0:T(8,128)(2,1)}, u32[]{:S(2)}, u32[]{:S(2)}) %all-to-all-start) | async-done | bytes 4194336 | tf_op jit(solution)/shard_map/all_to_all | solution.py:183
  96.2 74.6 %all-to-all-done.1 = bf16[4,2,256,1024]{3,2,1,0:T(8,128)(2,1)} async-done(((bf16[4,2,256,1024]{3,2,1,0:T(8,128)(2,1)}), bf16[4,2,256,1024]{3,2,1,0:T(8,128)(2,1)}, u32[]{:S(2)}, u32[]{:S(2)}) %all-to-all-start.1) | async-done | bytes 4194336 | tf_op jit(solution)/shard_map/all_to_all | solution.py:131
  175.5 12.5 fusion.77
  198.1 19.8 fusion.39
  288.0 630.3 %custom-call.10 = f32[16,2,2,1,128,128]{4,5,3,2,1,0:T(8,128)} custom-call(f32[16,2,2,1,128,128]{5,4,3,2,1,0:T(8,128)} %get-tuple-element.725), custom_call_target="InvertDiagBlocksLowerTriangular" | custom-call | tf_op jit(solution)/shard_map/jvp(jit(_solve_triangular))/vmap(vmap(vmap()))/triangular_solve | solution.py:77
  947.9 71.1 %while.38 = (s32[]{:T(128)}, f32[2,2,128,128]{3,2,1,0:T(8,128)S(1)}, f32[16,2,2,128,128]{4,3,2,1,0:T(8,128)}, f32[16,2,2,128,128]{4,3,2,1,0:T(8,128)}, f32[16,2,...) while((s32[]{:T(128)}, ...), condition=%wide.region_6.7_spmd.clone, body=%wide.region_5.6_spmd.clone.sunk | while | flops 201719808 | bytes 2885797 | solution.py:86
  1025.6 12.5 fusion.129
  1075.4 153.6 %all-reduce.36.cloned.1.call-done = bf16[2,1024,1024]{2,0,1:T(2,128)(2,1)} async-done(((bf16[2,1024,1024]{2,0,1:T(2,128)(2,1)}), bf16[2,1024,1024]{2,0,1:T(2,128)(2,1)}) %all-reduce.36.cloned.1.call-update) | async-done | bytes 4194320
  1246.8 141.1 %all-to-all-done.2 = bf16[4,2,256,1024]{3,2,1,0:T(8,128)(2,1)} async-done(((bf16[4,2,256,1024]{3,2,1,0:T(8,128)(2,1)}), bf16[4,2,256,1024]{3,2,1,0:T(8,128)(2,1)}, u32[]{:S(2)}, u32[]{:S(2)}) %all-to-all-start.2) | async-done | bytes 4194336 | tf_op jit(solution)/shard_map/all_to_all | solution.py:131
  1392.6 11.5 fusion.80
  1404.1 11.4 multiply_bitcast_fusion
  1419.8 22.7 bitcast_convert_fusion.1
  1451.1 155.4 %all-reduce.38.cloned.1.call-done = bf16[2,1024,1024]{2,0,1:T(2,128)(2,1)} async-done(((bf16[2,1024,1024]{2,0,1:T(2,128)(2,1)}), bf16[2,1024,1024]{2,0,1:T(2,128)(2,1)}) %all-reduce.38.cloned.1.call-update) | async-done | bytes 4194320
  1635.5 57.9 %all-gather.14.cloned.1.call-done = bf16[2,1024,1024]{2,0,1:T(2,128)(2,1)} async-done(((bf16[2,256,1024]{2,0,1:T(2,128)(2,1)}), bf16[2,1024,1024]{2,0,1:T(2,128)(2,1)}) %all-gather.14.cloned.1.call-update) | async-done | bytes 4194320 | tf_op jit(solution)/shard_map/all_gather | solution.py:142
  1747.8 153.8 %while.39 = (s32[]{:T(128)}, f32[2,2,128,128]{3,2,1,0:T(8,128)S(1)}, f32[16,2,2,128,128]{4,3,2,1,0:T(8,128)}, f32[16,2,2,128,128]{4,3,2,1,0:T(8,128)}, f32[16,2,...) while((s32[]{:T(128)}, ...), condition=%wide.region_19.20_spmd.clone, body=%wide.region_17.19_spmd.clone.sunk | while | flops 403439616 | bytes 4726519 | solution.py:86
  1901.6 16.4 fusion.48
  1918.0 12.4 fusion.49
  1930.4 19.8 multiply_reduce_fusion.6
  1950.2 14.0 fusion.90
  1973.0 11.9 add_add_fusion.1
  2071.8 24.4 multiply_reduce_fusion.2
  2096.2 14.5 broadcast_multiply_fusion
  2110.8 16.2 pad_add_fusion.2
  2130.8 25.9 bitcast_convert_fusion
  2171.0 23.0 bitcast_convert_fusion.4
  2198.7 255.1 %all-reduce.40.cloned.1.call-done = (bf16[2,1024,1024]{2,0,1:T(2,128)(2,1)}, bf16[2,1024,1024]{2,0,1:T(2,128)(2,1)}) async-done(((bf16[2,1024,1024]{2,0,1:T(2,128)(2,1)}, bf16[2,1024,1024]{2,0,1:T(2,128)(2,1)}), (bf16[2,1024,1024]{2,0,1:T(2,128)(2,1)}, bf16[2,1024,1024]{2,0,1:T(2,128)(2,1)})) %all-reduce.40.cloned.1.call-update) | async-done | bytes 8388624
  2478.0 27.3 bitcast_convert_fusion.3
  2535.3 56.1 %reduce-scatter.17.cloned.1.call-done = bf16[128,1408]{1,0:T(8,128)(2,1)} async-done(((bf16[1024,1408]{1,0:T(8,128)(2,1)}), bf16[128,1408]{1,0:T(8,128)(2,1)}) %reduce-scatter.17.cloned.1.call-update) | async-done | bytes 360464
  2594.9 33.7 %reduce-scatter.15.cloned.1.call-done = bf16[128,256]{1,0:T(8,128)(2,1)} async-done(((bf16[1024,256]{1,0:T(8,128)(2,1)}), bf16[128,256]{1,0:T(8,128)(2,1)}) %reduce-scatter.15.cloned.1.call-update) | async-done | bytes 65552
  2630.3 49.2 %reduce-scatter.13.cloned.1.call-done = bf16[128,1542]{1,0:T(8,128)(2,1)} async-done(((bf16[1024,1542]{1,0:T(8,128)(2,1)}), bf16[128,1542]{1,0:T(8,128)(2,1)}) %reduce-scatter.13.cloned.1.call-update) | async-done | bytes 394768
  2682.8 39.5 %all-reduce.27 = (f32[1024]{0:T(1024)}, f32[8]{0:T(128)}, f32[8]{0:T(128)}, f32[128]{0:T(128)}, f32[1024]{0:T(1024)}) all-reduce(f32[1024]{0:T(1024)S(1)} %get-tuple-element.635, f32[8]{0:T(128)S(1)} %multiply_dynamic-update-slice_fusion, f32[8]{0:T(128)S(1)} %dynamic_update_slice.55, ...), channel_id=1, replica_groups=mesh['fsdp'=8,'tp'=4] {'fsdp','tp'}, use_global_device_ids=true, to_apply=%region_33.34 | all-reduce | flops 2192 | bytes 17536 | tf_op jit(solution)/shard_map/psum | solution.py:295
  2734.9 74.1 %all-reduce.34.cloned.1.call-done = f32[8,640,4]{1,2,0:T(4,128)} async-done(((f32[8,640,4]{1,2,0:T(4,128)}), f32[8,640,4]{1,2,0:T(4,128)}) %all-reduce.34.cloned.1.call-update) | async-done | bytes 81936 | tf_op jit(solution)/shard_map/psum | solution.py:295
  (638 shorter events, 734.6 us)
Async XLA Ops:
  14.8 53.8 %all-to-all-start = ((bf16[8,256,1024]{2,1,0:T(8,128)(2,1)}), bf16[8,256,1024]{2,1,0:T(8,128)(2,1)}, u32[]{:S(2)}, u32[]{:S(2)}) async-start(bf16[8,256,1024]{2,1,0:T(8,128)(2,1)} %copy.604), calls=%async_computation | async-start | bytes 8388608 | tf_op jit(solution)/shard_map/all_to_all | solution.py:183
  73.9 1536.7 %copy-start.6 = (f32[2,256,1024]{2,0,1:T(2,128)}, f32[2,256,1024]{2,0,1:T(2,128)S(1)}, u32[]{:S(2)}) copy-start(f32[2,256,1024]{2,0,1:T(2,128)S(1)} %get-tuple-element.732) | copy-start | bytes 6291460
  78.4 92.4 %all-to-all-start.1 = ((bf16[4,2,256,1024]{3,2,1,0:T(8,128)(2,1)}), bf16[4,2,256,1024]{3,2,1,0:T(8,128)(2,1)}, u32[]{:S(2)}, u32[]{:S(2)}) async-start(bf16[4,2,256,1024]{3,2,1,0:T(8,128)(2,1)} %stack.4), calls=%async_computation.1 | async-start | bytes 8388608 | tf_op jit(solution)/shard_map/all_to_all | solution.py:131
  83.9 91.6 %all-gather.6.cloned.1.call-start = ((), (), s32[]{:S(2)}) async-start(), calls=%async_computation.9 | async-start | bytes 3575808 | tf_op jit(solution)/shard_map/all_gather | solution.py:196
  84.7 1144.3 %all-reduce.36.cloned.1.call-start = ((), (), s32[]{:S(2)}) async-start(), calls=%async_computation.19 | async-start | bytes 8388608
  228.9 713.1 %copy-start.84 = (f32[16,2,2,1]{0,2,3,1:T(2,128)}, f32[16,2,2,1]{0,2,3,1:T(2,128)S(1)}, u32[]{:S(2)}) copy-start(f32[16,2,2,1]{0,2,3,1:T(2,128)S(1)} %copy.765) | copy-start | bytes 772
  230.7 788.4 %copy-start.51 = (f32[2,1024,2]{1,2,0:T(2,128)}, f32[2,1024,2]{1,2,0:T(2,128)S(1)}, u32[]{:S(2)}) copy-start(f32[2,1024,2]{1,2,0:T(2,128)S(1)} %multiply_reduce_fusion.14) | copy-start | bytes 49156
  279.8 638.8 %copy-start.30 = (f32[2,16,64,2,2]{1,4,2,3,0:T(2,128)}, f32[2,16,64,2,2]{1,4,2,3,0:T(2,128)S(1)}, u32[]{:S(2)}) copy-start(f32[2,16,64,2,2]{1,4,2,3,0:T(2,128)S(1)} %copy.625) | copy-start | bytes 98308
  1072.9 319.7 %all-gather.8.cloned.1.call-start = ((), (), s32[]{:S(2)}) async-start(), calls=%async_computation.10 | async-start | bytes 3244032 | tf_op jit(solution)/shard_map/all_gather | solution.py:215
  1073.6 330.5 %all-gather.10.cloned.1.call-start = ((), (), s32[]{:S(2)}) async-start(), calls=%async_computation.11 | async-start | bytes 1622016 | tf_op jit(solution)/shard_map/all_gather | solution.py:216
  1231.0 379.6 %copy-start.17 = (bf16[2,256,1024]{2,0,1:T(2,128)(2,1)}, bf16[2,256,1024]{2,0,1:T(2,128)(2,1)S(1)}, u32[]{:S(2)}) copy-start(bf16[2,256,1024]{2,0,1:T(2,128)(2,1)S(1)} %constant_dynamic-slice_fusion.10) | copy-start | bytes 3145732
  1231.9 378.7 %copy-start.66 = (f32[2,256]{1,0:T(2,128)}, f32[2,256]{1,0:T(2,128)S(1)}, u32[]{:S(2)}) copy-start(f32[2,256]{1,0:T(2,128)S(1)} %fusion.201) | copy-start | bytes 6148
  1235.2 152.8 %all-to-all-start.2 = ((bf16[4,2,256,1024]{3,2,1,0:T(8,128)(2,1)}), bf16[4,2,256,1024]{3,2,1,0:T(8,128)(2,1)}, u32[]{:S(2)}, u32[]{:S(2)}) async-start(bf16[4,2,256,1024]{3,2,1,0:T(8,128)(2,1)} %stack.5), calls=%async_computation.2 | async-start | bytes 8388608 | tf_op jit(solution)/shard_map/all_to_all | solution.py:131
  1243.2 160.9 %all-gather.12.cloned.1.call-start = ((), (), s32[]{:S(2)}) async-start(), calls=%async_computation.12 | async-start | bytes 5242880 | tf_op jit(solution)/shard_map/all_gather | solution.py:142
  1243.2 367.4 %copy-start.78 = (f32[2,256]{1,0:T(2,128)}, f32[2,256]{1,0:T(2,128)S(1)}, u32[]{:S(2)}) copy-start(f32[2,256]{1,0:T(2,128)S(1)} %compare_convert_fusion) | copy-start | bytes 6148
  1246.8 359.7 %all-reduce.38.cloned.1.call-start = ((), (), s32[]{:S(2)}) async-start(), calls=%async_computation.20 | async-start | bytes 8388608
  1451.0 242.3 %all-gather.14.cloned.1.call-start = ((), (), s32[]{:S(2)}) async-start(), calls=%async_computation.13 | async-start | bytes 5242880 | tf_op jit(solution)/shard_map/all_gather | solution.py:142
  1613.9 839.9 %all-reduce.40.cloned.1.call-start = ((), (), s32[]{:S(2)}) async-start(), calls=%async_computation.21 | async-start | bytes 16777216
  2163.1 370.4 %reduce-scatter.19.cloned.1.call-start = ((), (), s32[]{:S(2)}) async-start(), calls=%async_computation.18 | async-start | bytes 1769472
  2171.0 420.4 %reduce-scatter.17.cloned.1.call-start = ((), (), s32[]{:S(2)}) async-start(), calls=%async_computation.17 | async-start | bytes 3244032
  2198.6 259.3 %copy-start.81 = (f32[2,256]{1,0:T(2,128)S(1)}, f32[2,256]{1,0:T(2,128)}, u32[]{:S(2)}) copy-start(f32[2,256]{1,0:T(2,128)} %copy-done.80) | copy-start | bytes 6148
  2198.6 260.5 %copy-start.83 = (f32[2,256]{1,0:T(2,128)S(1)}, f32[2,256]{1,0:T(2,128)}, u32[]{:S(2)}) copy-start(f32[2,256]{1,0:T(2,128)} %copy-done.82) | copy-start | bytes 6148
  2198.6 260.5 %copy-start.18 = (bf16[2,256,1024]{2,0,1:T(2,128)(2,1)S(1)}, bf16[2,256,1024]{2,0,1:T(2,128)(2,1)}, u32[]{:S(2)}) copy-start(bf16[2,256,1024]{2,0,1:T(2,128)(2,1)} %copy-done.17) | copy-start | bytes 3145732
  2198.6 260.5 %copy-start.65 = (f32[1024]{0:T(1024)S(1)}, f32[1024]{0:T(1024)}, u32[]{:S(2)}) copy-start(f32[1024]{0:T(1024)} %param.29) | copy-start | bytes 12292
  2198.6 260.5 %copy-start.67 = (f32[2,256]{1,0:T(2,128)S(1)}, f32[2,256]{1,0:T(2,128)}, u32[]{:S(2)}) copy-start(f32[2,256]{1,0:T(2,128)} %copy-done.66) | copy-start | bytes 6148
  2198.7 260.5 %copy-start.79 = (f32[2,256]{1,0:T(2,128)S(1)}, f32[2,256]{1,0:T(2,128)}, u32[]{:S(2)}) copy-start(f32[2,256]{1,0:T(2,128)} %copy-done.78) | copy-start | bytes 6148
  2198.7 260.5 %copy-start.87 = (f32[2,256]{1,0:T(2,128)S(1)}, f32[2,256]{1,0:T(2,128)}, u32[]{:S(2)}) copy-start(f32[2,256]{1,0:T(2,128)} %copy-done.86) | copy-start | bytes 6148
  2468.2 60.3 %all-to-all-start.4 = ((bf16[8,256,1024]{2,1,0:T(8,128)(2,1)}), bf16[8,256,1024]{2,1,0:T(8,128)(2,1)}, u32[]{:S(2)}, u32[]{:S(2)}) async-start(bf16[8,256,1024]{2,1,0:T(8,128)(2,1)} %copy.712), calls=%async_computation.4 | async-start | bytes 8388608 | tf_op jit(solution)/shard_map/all_to_all | solution.py:307
  2473.1 155.6 %reduce-scatter.15.cloned.1.call-start = ((), (), s32[]{:S(2)}) async-start(), calls=%async_computation.16 | async-start | bytes 589824
  2478.0 201.5 %reduce-scatter.13.cloned.1.call-start = ((), (), s32[]{:S(2)}) async-start(), calls=%async_computation.15 | async-start | bytes 3833856
  2528.5 198.9 %all-to-all-start.3 = ((bf16[8,256,1024]{2,1,0:T(8,128)(2,1)}), bf16[8,256,1024]{2,1,0:T(8,128)(2,1)}, u32[]{:S(2)}, u32[]{:S(2)}) async-start(bf16[8,256,1024]{2,1,0:T(8,128)(2,1)} %copy.651), calls=%async_computation.3 | async-start | bytes 8388608 | tf_op jit(solution)/shard_map/all_to_all | solution.py:306
  2533.2 275.8 %all-reduce.34.cloned.1.call-start = ((), (), s32[]{:S(2)}) async-start(), calls=%async_computation.14 | async-start | bytes 163840 | tf_op jit(solution)/shard_map/psum | solution.py:295
  (94 other events, 3298.8 us)
Sparse Core Ops, SparseCore 0:
  87.2 32.0 all-gather.5
  1073.0 155.9 all-reduce.35
  1231.1 32.8 all-gather.7
  1265.8 25.2 all-gather.9
  1293.2 107.5 all-gather.11
  1451.2 155.2 all-reduce.37
  1614.1 79.2 all-gather.13
  2163.2 290.5 all-reduce.39
  2457.1 52.8 reduce-scatter.18
  2513.2 78.1 reduce-scatter.16
  2595.4 33.2 reduce-scatter.14
  2632.0 47.4 reduce-scatter.12
  2686.6 122.3 all-reduce.33
